TPU v7x, 256 devices: a whole 4x4x8 slice. The times are simulated.
256 devices in a mesh: inner: 32 (over z_lo, y, core), outer: 8 (over x, z_hi).
Axes of the slice: x: 4, y: 4, z: 8 (z_hi: 2, z_lo: 4; z = z_hi * 4 + z_lo), core: 2. Of those that a mesh axis runs over, the one named last changes fastest.
Arguments:
- activations: bfloat16 [65536, 512], P(('inner', 'outer')), may hold values from -12 to 12
- cotangent: bfloat16 [65536, 14336], P(('inner', 'outer')), may hold values from -0.046875 to 0.046875
Outputs:
- weight_grad: float32 [512, 14336], P(('inner', 'outer'))
All inputs are finite; a program needn't handle non-finite values.
Results may differ from a plain program's by a relative error of at most 0.014.
Values may be sent and summed in bfloat16 or wider, within the bound.
A program may use at most 192 MiB of HBM per device.

v0:
```python
import math

import jax
import jax.numpy as jnp
from jax import lax
from jax.sharding import PartitionSpec as P

epsilon = 1e-06
code_range = 448.0
clip_ratio = 2.0


def as_sent(x):
    return jax.tree.map(lambda a: a.astype(jnp.bfloat16) if a.dtype == jnp.float32 else a, x)


def hadamard():
    indices = jnp.arange(128, dtype=jnp.int32)
    common_bits = indices[:, None] & indices[None, :]
    bit_count = jnp.zeros((128, 128), jnp.int32)
    for shift_by in range(7):
        bit_count = bit_count + (common_bits >> shift_by & 1)
    signs = 1 - 2 * (bit_count % 2)
    return signs.astype(jnp.float32) / math.sqrt(128.0)


def rotate(blocks, hadamard_matrix):
    return jnp.einsum("rbk,kj->rbj", blocks, hadamard_matrix, precision=lax.Precision.HIGHEST)


def quantize(blocks):
    mean_square = jnp.mean(blocks * blocks, axis=-1)
    block_scale = clip_ratio * jnp.sqrt(mean_square + epsilon) / code_range
    coded = jnp.clip(blocks / block_scale[..., None], -code_range, code_range).astype(jnp.bfloat16)
    return (coded, block_scale)


def dequantize(coded, block_scale):
    return coded.astype(jnp.float32) * block_scale[..., None]


def gradient_codes(activations, cot_columns, hadamard_matrix):
    local_grad = lax.dot_general(
        activations, cot_columns, (((0,), (0,)), ((), ())), preferred_element_type=jnp.float32
    )
    blocks = local_grad.reshape(local_grad.shape[0], local_grad.shape[1] // 128, 128)
    return quantize(rotate(blocks, hadamard_matrix))


def combine_group(received):
    coded, block_scale = received
    partial_value = jnp.sum(dequantize(coded, block_scale), axis=0)
    return quantize(partial_value)


def on_device(activations, cotangent):
    hadamard_matrix = hadamard()
    inner_count = lax.axis_size("inner")
    outer_count = lax.axis_size("outer")
    grad_rows = activations.shape[1]
    grad_cols = cotangent.shape[1]
    block_count = grad_cols // 128
    group_rows = grad_rows // inner_count
    owned_rows = group_rows // outer_count
    coded, block_scale = gradient_codes(activations, cotangent, hadamard_matrix)
    group_coded, group_scale = combine_group(
        (
            lax.all_to_all(
                coded.reshape(inner_count, group_rows, block_count, 128),
                "inner",
                split_axis=0,
                concat_axis=0,
                tiled=True,
            ),
            lax.all_to_all(
                block_scale.reshape(inner_count, group_rows, block_count).astype(jnp.bfloat16),
                "inner",
                split_axis=0,
                concat_axis=0,
                tiled=True,
            ).astype(jnp.float32),
        )
    )
    arrived_coded, arrived_scale = (
        lax.all_to_all(
            group_coded.reshape(outer_count, owned_rows, block_count, 128),
            "outer",
            split_axis=0,
            concat_axis=0,
            tiled=True,
        ),
        lax.all_to_all(
            as_sent(group_scale.reshape(outer_count, owned_rows, block_count)),
            "outer",
            split_axis=0,
            concat_axis=0,
            tiled=True,
        ),
    )
    summed = jnp.sum(dequantize(arrived_coded, arrived_scale), axis=0)
    return rotate(summed, hadamard_matrix).reshape(owned_rows, grad_cols)


def solution(mesh):
    placed = (P(("inner", "outer"), None), P(("inner", "outer"), None))
    return jax.shard_map(
        on_device,
        mesh=mesh,
        in_specs=placed,
        out_specs=P(("inner", "outer"), None),
        check_vma=False,
    )
```

profile of v0, /device:TPU:1, one launch (start us, length us, event | category | flops | bytes accessed | tf_op | source)
XLA Modules:
  0.0 471.9 jit_solution(4202573446953848054)
XLA Ops:
  0.0 0.9 copy-done
  1.0 14.7 %convolution_bitcast_fusion = f32[64,112,8,128]{3,2,1,0:T(8,128)} fusion(bf16[256,512]{1,0:T(8,128)(2,1)S(1)} %copy-done, bf16[256,14336]{1,0:T(8,128)(2,1)} %param.3), kind=kOutput, calls=%fused_computation.6 | convolution fusion | flops 3758096384 | bytes 36962304 | tf_op jit(solution)/shard_map/dot_general | solution.py:43
  15.6 29.3 %multiply_reduce_fusion.1 = (f32[512,112]{0,1:T(8,128)S(1)}, f32[512,112,128]{2,0,1:T(8,128)}) fusion(f32[64,112,8,128]{3,2,1,0:T(8,128)} %convolution_bitcast_fusion), kind=kOutput, calls=%fused_computation.5 | convolution fusion | flops 11289501696 | bytes 58949632 | tf_op jit(solution)/shard_map/rbk,kj->rbj/dot_general | solution.py:28
  44.9 0.1 fusion.43
  45.0 0.8 copy.45
  45.8 10.2 %all-to-all-start.1 = ((bf16[32,16,112]{2,1,0:T(8,128)(2,1)}), bf16[32,16,112]{2,1,0:T(8,128)(2,1)S(1)}, u32[]{:S(2)}, u32[]{:S(2)}) async-start(bf16[32,16,112]{2,1,0:T(8,128)(2,1)} %bitcast.2), calls=%async_computation.1 | async-start | bytes 262144 | tf_op jit(solution)/shard_map/all_to_all | solution.py:75
  56.0 15.8 %clamp_convert_fusion = bf16[512,112,128]{2,0,1:T(8,128)(2,1)} fusion(f32[512,112,128]{2,0,1:T(8,128)} %get-tuple-element.8, f32[512,112]{0,1:T(8,128)S(1)} %get-tuple-element.6), kind=kLoop, calls=%fused_computation.4 | loop fusion | flops 22020096 | bytes 44269568 | tf_op jit(solution)/shard_map/convert_element_type | solution.py:34
  71.8 14.8 %copy.44 = bf16[32,16,112,128]{3,1,2,0:T(8,128)(2,1)} copy(bf16[32,16,112,128]{3,1,0,2:T(8,128)(2,1)} %bitcast.28) | data formatting | bytes 29360128 | tf_op jit(solution)/shard_map/reshape | solution.py:69
  86.5 7.8 %all-to-all-start = ((bf16[32,16,112,128]{3,1,2,0:T(8,128)(2,1)}), bf16[32,16,112,128]{3,1,2,0:T(8,128)(2,1)}, u32[]{:S(2)}, u32[]{:S(2)}) async-start(bf16[32,16,112,128]{3,1,2,0:T(8,128)(2,1)} %copy.44), calls=%async_computation | async-start | bytes 29360128 | tf_op jit(solution)/shard_map/all_to_all | solution.py:68
  94.3 0.3 copy.46
  94.6 325.7 %all-to-all-done = bf16[32,16,112,128]{3,1,2,0:T(8,128)(2,1)} async-done(((bf16[32,16,112,128]{3,1,2,0:T(8,128)(2,1)}), bf16[32,16,112,128]{3,1,2,0:T(8,128)(2,1)}, u32[]{:S(2)}, u32[]{:S(2)}) %all-to-all-start) | async-done | bytes 14680096 | tf_op jit(solution)/shard_map/all_to_all | solution.py:68
  420.4 10.4 %multiply_reduce_fusion = f32[16,112,128]{2,0,1:T(8,128)S(1)} fusion(bf16[32,16,112,128]{3,1,2,0:T(8,128)(2,1)} %all-to-all-done, f32[32,16,112]{1,2,0:T(8,128)S(1)} %copy.46), kind=kLoop, calls=%fused_computation.3 | loop fusion | flops 21790720 | bytes 15826944 | tf_op jit(solution)/shard_map/reduce_sum | solution.py:52
  430.8 0.3 multiply_reduce_fusion.3
  431.1 0.3 copy.48
  431.5 0.6 convert_element_type.35
  432.1 12.5 %all-to-all-start.3 = ((bf16[8,2,112]{2,1,0:T(2,128)(2,1)}), bf16[8,2,112]{2,1,0:T(2,128)(2,1)S(1)}, u32[]{:S(2)}, u32[]{:S(2)}) async-start(bf16[8,2,112]{2,1,0:T(2,128)(2,1)} %convert_element_type.35), calls=%async_computation.3 | async-start | bytes 8192 | tf_op jit(solution)/shard_map/all_to_all | solution.py:92
  444.6 0.3 clamp_convert_fusion.1
  444.9 1.1 copy.50
  446.1 7.4 %all-to-all-done.3 = bf16[8,2,112]{2,1,0:T(2,128)(2,1)S(1)} async-done(((bf16[8,2,112]{2,1,0:T(2,128)(2,1)}), bf16[8,2,112]{2,1,0:T(2,128)(2,1)S(1)}, u32[]{:S(2)}, u32[]{:S(2)}) %all-to-all-start.3) | async-done | bytes 3616 | tf_op jit(solution)/shard_map/all_to_all | solution.py:92
  453.5 3.5 all-to-all-start.2
  457.0 13.6 %all-to-all-done.2 = bf16[8,2,112,128]{3,1,2,0:T(2,128)(2,1)S(1)} async-done(((bf16[8,2,112,128]{3,1,2,0:T(2,128)(2,1)}), bf16[8,2,112,128]{3,1,2,0:T(2,128)(2,1)S(1)}, u32[]{:S(2)}, u32[]{:S(2)}) %all-to-all-start.2) | async-done | bytes 458784 | tf_op jit(solution)/shard_map/all_to_all | solution.py:85
  470.6 0.3 multiply_reduce_fusion.2
  470.9 0.3 convolution_bitcast_fusion.1
  471.2 0.7 copy.70
  (8 shorter events, 0.1 us)
Async XLA Ops:
  0.0 1.0 copy-start
  45.8 40.7 %all-to-all-start.1 = ((bf16[32,16,112]{2,1,0:T(8,128)(2,1)}), bf16[32,16,112]{2,1,0:T(8,128)(2,1)S(1)}, u32[]{:S(2)}, u32[]{:S(2)}) async-start(bf16[32,16,112]{2,1,0:T(8,128)(2,1)} %bitcast.2), calls=%async_computation.1 | async-start | bytes 262144 | tf_op jit(solution)/shard_map/all_to_all | solution.py:75
  71.8 400.2 %copy-start.1 = (bf16[256,512]{1,0:T(8,128)(2,1)S(1)}, bf16[256,512]{1,0:T(8,128)(2,1)}, u32[]{:S(2)}) copy-start(bf16[256,512]{1,0:T(8,128)(2,1)} %param.2) | copy-start | bytes 786436
  86.5 333.8 %all-to-all-start = ((bf16[32,16,112,128]{3,1,2,0:T(8,128)(2,1)}), bf16[32,16,112,128]{3,1,2,0:T(8,128)(2,1)}, u32[]{:S(2)}, u32[]{:S(2)}) async-start(bf16[32,16,112,128]{3,1,2,0:T(8,128)(2,1)} %copy.44), calls=%async_computation | async-start | bytes 29360128 | tf_op jit(solution)/shard_map/all_to_all | solution.py:68
  432.1 21.3 %all-to-all-start.3 = ((bf16[8,2,112]{2,1,0:T(2,128)(2,1)}), bf16[8,2,112]{2,1,0:T(2,128)(2,1)S(1)}, u32[]{:S(2)}, u32[]{:S(2)}) async-start(bf16[8,2,112]{2,1,0:T(2,128)(2,1)} %convert_element_type.35), calls=%async_computation.3 | async-start | bytes 8192 | tf_op jit(solution)/shard_map/all_to_all | solution.py:92
  453.5 17.1 %all-to-all-start.2 = ((bf16[8,2,112,128]{3,1,2,0:T(2,128)(2,1)}), bf16[8,2,112,128]{3,1,2,0:T(2,128)(2,1)S(1)}, u32[]{:S(2)}, u32[]{:S(2)}) async-start(bf16[8,2,112,128]{3,1,2,0:T(2,128)(2,1)} %copy.50), calls=%async_computation.2 | async-start | bytes 917504 | tf_op jit(solution)/shard_map/all_to_all | solution.py:85
where the time goes:
time: 473 us; the launch traced here: 472 us
  waiting for transfers between devices  347 us (73%)
  matrix products  44.3 us (9%)
  starting transfers between devices  33.9 us (7%)
  other arithmetic  27.8 us (6%)
  local copies, waits for them, and re-layouts  19 us (4%)
    all_to_all x1, waiting for transfers between devices, on_device(): lax.all_to_all(coded.reshape(inner_count, group_rows, block_count, 128),...  326 us
    dot_general x2, matrix products, rotate(): jnp.einsum('rbk,kj->rbj', blocks, hadamard_matrix, precision=lax.Precisio...  29.6 us
    convert_element_type x2, other arithmetic, quantize(): jnp.clip(blocks / block_scale[..., None], -code_range, code_range)  16.1 us
    reshape x1, local copies, waits for them, and re-layouts, on_device(): coded.reshape(inner_count, group_rows, block_count, 128)  14.8 us
    dot_general x1, matrix products, gradient_codes(): lax.dot_general(activations, cot_columns, (((0,), (0,)), ((), ())), prefe...  14.7 us
    all_to_all x1, waiting for transfers between devices, on_device(): lax.all_to_all(group_coded.reshape(outer_count, owned_rows, block_count,...  13.6 us
    all_to_all x1, starting transfers between devices, on_device(): lax.all_to_all(as_sent(group_scale.reshape(outer_count, owned_rows, block...  12.5 us
    reduce_sum x1, other arithmetic, combine_group(): partial_value = jnp.sum(dequantize(coded, block_scale), axis=0)  10.4 us
  transfers between devices with their start and end apart: 4, of which 3 were waited for; matrix products, arithmetic and copies ran while one was open for 7% of the time, Pallas kernels for 0%

commit v1 on v0

v1 whole, which is shorter than its diff:
```python
import functools

import jax
import jax.numpy as jnp
from jax import lax
from jax.experimental import pallas as pl
from jax.experimental.pallas import tpu as pltpu
from jax.sharding import PartitionSpec as P

MESH = pl.DeviceIdType.MESH
epsilon = 1e-06
LANES = 128
y_jobs, y_width = 12, 4
z_jobs, z_width = 4, 2
round_blocks = 8
y_per_round = round_blocks // y_width
y_rounds = y_jobs * y_width // round_blocks
rounds = y_rounds + z_jobs * z_width // round_blocks
half_blocks = y_jobs * y_width + z_jobs * z_width
half_cols = half_blocks * LANES
WY, WZ = y_width * LANES, z_width * LANES
TOK, ROWS = 256, 512
f32, bf16 = jnp.float32, jnp.bfloat16


def near(v):
    return v + 1 - 2 * (v % 2)


def signs():
    r = lax.broadcasted_iota(jnp.int32, (256, 256), 0)
    q = lax.broadcasted_iota(jnp.int32, (256, 256), 1)
    common = r & q & 127
    common = common ^ (common >> 4)
    common = common ^ (common >> 2)
    common = common ^ (common >> 1)
    sign = (1 - 2 * (common & 1)).astype(f32)
    return jnp.where((r >> 7) == (q >> 7), sign, 0.0).astype(bf16)


def clipped(v):
    total = jnp.sum(v * v, axis=-1, keepdims=True)
    four = total * (4.0 / LANES) + 4.0 * LANES * epsilon
    bound = four * lax.rsqrt(four)
    return jnp.minimum(jnp.maximum(v, -bound), bound)


def kernel(act, cot, out, h2, at2, asib, cy_own, cy_sib, cz_own, cz_sib, ch, ty, tz,
           ry1a, ry1b, ry2a, ry2b, ry3, ry4, rz1, rz2, rz3a, rz3b, rz4a, rz4b,
           part_y, part_z, coded, arrived,
           s_loc, s_a, s_cot, s_y1, s_y2, s_y3, s_y4, s_z1, s_z2, s_z3, s_z4, s_out):
    i, o = lax.axis_index("inner"), lax.axis_index("outer")
    z, y, c = i // 8, (i // 2) % 4, i % 2
    yn, yf, yo = near(y), 3 - y, (y + 2) % 4
    zn, zf, zo = near(z), 3 - z, (z + 2) % 4

    def dev(z_, y_, c_, o_):
        return (z_ * 8 + y_ * 2 + c_, o_)

    sib = dev(z, y, 1 - c, o)
    dev_yn, dev_yf = dev(z, yn, c, o), dev(z, yf, c, o)
    dev_zn, dev_zf = dev(zn, y, c, o), dev(zf, y, c, o)
    mine = c * 8 + o

    def other(d):
        at = (mine + d) % 16
        return at, dev(z, y, at // 8, at % 8)

    def send(src, dst, sems, where, to):
        return pltpu.make_async_remote_copy(
            src_ref=src, dst_ref=dst, send_sem=sems.at[(0,) + where], recv_sem=sems.at[(1,) + where],
            device_id=to, device_id_type=MESH)

    barrier = pltpu.get_barrier_semaphore()

    def greet(d, _):
        pl.semaphore_signal(barrier, inc=1, device_id=other(d)[1], device_id_type=MESH)
        return 0

    for to in (dev_yn, dev_yf, dev_zn, dev_zf):
        pl.semaphore_signal(barrier, inc=1, device_id=to, device_id_type=MESH)
    lax.fori_loop(1, 16, greet, 0)

    def y_cols(half, j):
        return pl.ds(pl.multiple_of(half * half_cols + j * WY, LANES), WY)

    def z_cols(half, j):
        return pl.ds(pl.multiple_of(half * half_cols + y_jobs * WY + j * WZ, LANES), WZ)

    def load_y(j):
        return pltpu.make_async_copy(cot.at[:, y_cols(c, j)], cy_own.at[j], s_loc.at[j])

    def load_z(j):
        return pltpu.make_async_copy(cot.at[:, z_cols(c, j)], cz_own.at[j], s_loc.at[y_jobs + j])

    def lend_y(j):
        return send(cot.at[:, y_cols(1 - c, j)], cy_sib.at[j], s_cot, (j,), sib)

    def lend_z(j):
        return send(cot.at[:, z_cols(1 - c, j)], cz_sib.at[j], s_cot, (y_jobs + j,), sib)

    def each(n, f):
        def step(j, _):
            f(j)
            return 0
        lax.fori_loop(0, n, step, 0)

    def start_loads(j):
        load_y(j).start()

        @pl.when(j < z_jobs)
        def _():
            load_z(j).start()

    def start_lends(j):
        lend_y(j).start()

        @pl.when(j < z_jobs)
        def _():
            lend_z(j).start()

    each(y_jobs, start_loads)
    h2[...] = signs()

    def turn(which, a):
        t = a.astype(f32).T.astype(bf16)
        at2[which, :, 0:TOK] = t
        at2[which, :, TOK:2 * TOK] = t

    turn(0, act[...])
    pl.semaphore_wait(barrier, 19)
    lend_a = send(act, asib, s_a, (), sib)
    lend_a.start()
    each(y_jobs, start_lends)
    lend_a.wait_recv()
    turn(1, asib[...])

    def compute(own, other_, t, width):
        for which, block in ((0, own), (1, other_)):
            for p in range(width // 256):
                cols = slice(p * 256, p * 256 + 256)
                v = jnp.dot(block[:, cols], h2[...], preferred_element_type=f32)
                hi = v.astype(bf16)
                ch[which, 0:TOK, cols] = hi
                ch[which, TOK:2 * TOK, cols] = (v - hi.astype(f32)).astype(bf16)

        def rows(q, _):
            at = pl.ds(pl.multiple_of(q * 256, 256), 256)
            for p in range(width // 256):
                cols = slice(p * 256, p * 256 + 256)
                a = jnp.dot(at2[0, at, :], ch[0, :, cols], preferred_element_type=f32)
                b = jnp.dot(at2[1, at, :], ch[1, :, cols], preferred_element_type=f32)
                for k in range(2):
                    lanes = slice(k * LANES, k * LANES + LANES)
                    s = (clipped(a[:, lanes]) + clipped(b[:, lanes])).astype(bf16)
                    to = slice(p * 256 + k * LANES, p * 256 + k * LANES + LANES)
                    for zz in range(2):
                        for yy in range(4):
                            t[yy, q * 2 + zz, :, to] = s[zz * 128 + yy * 32:zz * 128 + yy * 32 + 32]
            return 0

        lax.fori_loop(0, 2, rows, 0)

    lo, hi_ = pl.ds(0, 2), pl.ds(2, 2)

    def y1(j):
        return (send(ty.at[j, yo, lo], ry1a.at[j, 1], s_y1, (j, 0), dev_yn),
                send(ty.at[j, yo, hi_], ry1b.at[j, 1], s_y1, (j, 1), dev_yf),
                send(ty.at[j, yn, lo], ry1a.at[j, 0], s_y1, (j, 2), dev_yn),
                send(ty.at[j, yf, hi_], ry1b.at[j, 0], s_y1, (j, 3), dev_yf))

    def y2(j):
        return (send(ty.at[j, yf, lo], ry2a.at[j], s_y2, (j, 0), dev_yf),
                send(ty.at[j, yn, hi_], ry2b.at[j], s_y2, (j, 1), dev_yn))

    def y3(j):
        return (send(ty.at[j, y, zo], ry3.at[j, 1], s_y3, (j, 0), dev_zn),
                send(ty.at[j, y, zn], ry3.at[j, 0], s_y3, (j, 1), dev_zn))

    def y4(j):
        return (send(ty.at[j, y, zf], ry4.at[j], s_y4, (j,), dev_zf),)

    def start(copies):
        for cp in copies:
            cp.start()

    def y_stage0(j):
        load_y(j).wait()
        lend_y(j).wait_recv()
        compute(cy_own.at[j], cy_sib.at[j], ty.at[j], WY)
        start(y1(j))

    def y_stage1(j):
        first_a, first_b, last_a, last_b = y1(j)
        second_a, second_b = y2(j)
        first_a.wait_recv()
        ty[j, yf, 0:2] = ty[j, yf, 0:2] + ry1a[j, 1]
        second_a.start()
        first_b.wait_recv()
        ty[j, yn, 2:4] = ty[j, yn, 2:4] + ry1b[j, 1]
        second_b.start()
        last_a.wait_recv()
        ty[j, y, 0:2] = ty[j, y, 0:2] + ry1a[j, 0]
        last_b.wait_recv()
        ty[j, y, 2:4] = ty[j, y, 2:4] + ry1b[j, 0]

    def y_stage2(j):
        a, b = y2(j)
        a.wait_recv()
        ty[j, y, 0:2] = ty[j, y, 0:2] + ry2a[j]
        b.wait_recv()
        ty[j, y, 2:4] = ty[j, y, 2:4] + ry2b[j]
        start(y3(j))

    def y_stage3(j):
        first, last = y3(j)
        first.wait_recv()
        ty[j, y, zf] = ty[j, y, zf] + ry3[j, 1]
        start(y4(j))
        last.wait_recv()
        ty[j, y, z] = ty[j, y, z] + ry3[j, 0]

    def out_copy(g, d):
        at, to = other(d)
        return send(coded.at[g, at], arrived.at[g, mine], s_out, (g, d), to)

    def send_round(g, part):
        for d in range(16):
            rows = [part[pl.ds(2 * d + e, round_blocks, stride=32), :] for e in range(2)]
            coded[g, d] = jnp.concatenate(rows, axis=0).astype(bf16)

        def go(d, _):
            out_copy(g, d).start()
            return 0

        lax.fori_loop(1, 16, go, 0)
        arrived[g, mine] = coded[g, mine]

    def y_stage4(j):
        y4(j)[0].wait_recv()
        v = ty[j, y, z].astype(f32) + ry4[j].astype(f32)
        for k in range(y_width):
            to = pl.multiple_of((j % y_per_round) * (y_width * 32) + k * 32, 32)
            part_y[pl.ds(to, 32), :] = clipped(v[:, k * LANES:(k + 1) * LANES])

        @pl.when(j % y_per_round == y_per_round - 1)
        def _():
            send_round(j // y_per_round, part_y)

    top, bottom = pl.ds(0, 16), pl.ds(16, 16)

    def z1(j):
        return (send(tz.at[j, :, zo], rz1.at[j, 1], s_z1, (j, 0), dev_zn),
                send(tz.at[j, :, zn], rz1.at[j, 0], s_z1, (j, 1), dev_zn))

    def z2(j):
        return (send(tz.at[j, :, zf], rz2.at[j], s_z2, (j,), dev_zf),)

    def z3(j):
        return (send(tz.at[j, yo, z, top], rz3a.at[j, 1], s_z3, (j, 0), dev_yn),
                send(tz.at[j, yo, z, bottom], rz3b.at[j, 1], s_z3, (j, 1), dev_yf),
                send(tz.at[j, yn, z, top], rz3a.at[j, 0], s_z3, (j, 2), dev_yn),
                send(tz.at[j, yf, z, bottom], rz3b.at[j, 0], s_z3, (j, 3), dev_yf))

    def z4(j):
        return (send(tz.at[j, yf, z, top], rz4a.at[j], s_z4, (j, 0), dev_yf),
                send(tz.at[j, yn, z, bottom], rz4b.at[j], s_z4, (j, 1), dev_yn))

    def z_stage0(j):
        load_z(j).wait()
        lend_z(j).wait_recv()
        compute(cz_own.at[j], cz_sib.at[j], tz.at[j], WZ)
        start(z1(j))

    def z_stage1(j):
        first, last = z1(j)
        first.wait_recv()
        tz[j, :, zf] = tz[j, :, zf] + rz1[j, 1]
        start(z2(j))
        last.wait_recv()
        tz[j, :, z] = tz[j, :, z] + rz1[j, 0]

    def z_stage2(j):
        z2(j)[0].wait_recv()
        tz[j, :, z] = tz[j, :, z] + rz2[j]
        start(z3(j))

    def z_stage3(j):
        first_a, first_b, last_a, last_b = z3(j)
        second_a, second_b = z4(j)
        first_a.wait_recv()
        tz[j, yf, z, 0:16] = tz[j, yf, z, 0:16] + rz3a[j, 1]
        second_a.start()
        first_b.wait_recv()
        tz[j, yn, z, 16:32] = tz[j, yn, z, 16:32] + rz3b[j, 1]
        second_b.start()
        last_a.wait_recv()
        tz[j, y, z, 0:16] = tz[j, y, z, 0:16] + rz3a[j, 0]
        last_b.wait_recv()
        tz[j, y, z, 16:32] = tz[j, y, z, 16:32] + rz3b[j, 0]

    def z_stage4(j):
        a, b = z4(j)
        a.wait_recv()
        b.wait_recv()
        v = tz[j, y, z].astype(f32)
        v = v + jnp.concatenate([rz4a[j], rz4b[j]], axis=0).astype(f32)
        for k in range(z_width):
            to = pl.multiple_of(j * (z_width * 32) + k * 32, 32)
            part_z[pl.ds(to, 32), :] = clipped(v[:, k * LANES:(k + 1) * LANES])

        @pl.when(j == z_jobs - 1)
        def _():
            send_round(y_rounds, part_z)

    def finish(g):
        def take(d, _):
            out_copy(g, d).wait_recv()
            return 0

        lax.fori_loop(1, 16, take, 0)
        for half in range(2):
            total = arrived[g, half * 8].astype(f32)
            for k in range(1, 8):
                total = total + arrived[g, half * 8 + k].astype(f32)
            hi = total.astype(bf16)
            rest = (total - hi.astype(f32)).astype(bf16)
            h = h2[0:LANES, 0:LANES]
            v = jnp.dot(hi, h, preferred_element_type=f32) + jnp.dot(rest, h, preferred_element_type=f32)
            v = v * (1.0 / LANES)
            to = pl.ds(pl.multiple_of(half * half_blocks + g * round_blocks, 8), round_blocks)
            out[0, to, :] = v[0:8]
            out[1, to, :] = v[8:16]

    def tick(t, _):
        def at(stage, jobs, f):
            @pl.when((t >= stage) & (t < jobs + stage))
            def _():
                f(t - stage)

        at(0, y_jobs, y_stage0)
        at(0, z_jobs, z_stage0)
        at(1, y_jobs, y_stage1)
        at(1, z_jobs, z_stage1)
        at(2, y_jobs, y_stage2)
        at(2, z_jobs, z_stage2)
        at(3, y_jobs, y_stage3)
        at(3, z_jobs, z_stage3)
        at(4, y_jobs, y_stage4)
        at(4, z_jobs, z_stage4)
        return 0

    lax.fori_loop(0, y_jobs + 4, tick, 0)
    finish(y_rounds)
    each(y_rounds, finish)

    lend_a.wait_send()

    def drain_y(j):
        for cp in (lend_y(j),) + y1(j) + y2(j) + y3(j) + y4(j):
            cp.wait_send()

    def drain_z(j):
        for cp in (lend_z(j),) + z1(j) + z2(j) + z3(j) + z4(j):
            cp.wait_send()

    each(y_jobs, drain_y)
    each(z_jobs, drain_z)

    def drain_round(g):
        def gone(d, _):
            out_copy(g, d).wait_send()
            return 0
        lax.fori_loop(1, 16, gone, 0)

    each(rounds, drain_round)


def on_device(activations, cotangent):
    dma = pltpu.SemaphoreType.DMA
    vm = pltpu.VMEM
    ny, nz = y_jobs, z_jobs
    out = pl.pallas_call(
        kernel,
        out_shape=jax.ShapeDtypeStruct((2, 2 * half_blocks, LANES), f32),
        in_specs=[pl.BlockSpec(memory_space=pltpu.VMEM), pl.BlockSpec(memory_space=pl.ANY)],
        out_specs=pl.BlockSpec(memory_space=pltpu.VMEM),
        scratch_shapes=[
            vm((256, 256), bf16),
            vm((2, ROWS, 2 * TOK), bf16),
            vm((TOK, ROWS), bf16),
            vm((ny, TOK, WY), bf16), vm((ny, TOK, WY), bf16),
            vm((nz, TOK, WZ), bf16), vm((nz, TOK, WZ), bf16),
            vm((2, 2 * TOK, max(WY, WZ)), bf16),
            vm((ny, 4, 4, 32, WY), bf16),
            vm((nz, 4, 4, 32, WZ), bf16),
            vm((ny, 2, 2, 32, WY), bf16), vm((ny, 2, 2, 32, WY), bf16),
            vm((ny, 2, 32, WY), bf16), vm((ny, 2, 32, WY), bf16),
            vm((ny, 2, 32, WY), bf16), vm((ny, 32, WY), bf16),
            vm((nz, 2, 4, 32, WZ), bf16), vm((nz, 4, 32, WZ), bf16),
            vm((nz, 2, 16, WZ), bf16), vm((nz, 2, 16, WZ), bf16),
            vm((nz, 16, WZ), bf16), vm((nz, 16, WZ), bf16),
            vm((32 * round_blocks, LANES), f32), vm((32 * round_blocks, LANES), f32),
            vm((rounds, 16, 16, LANES), bf16), vm((rounds, 16, 16, LANES), bf16),
            dma((ny + nz,)), dma((2,)), dma((2, ny + nz)),
            dma((2, ny, 4)), dma((2, ny, 2)), dma((2, ny, 2)), dma((2, ny)),
            dma((2, nz, 2)), dma((2, nz)), dma((2, nz, 4)), dma((2, nz, 2)),
            dma((2, rounds, 16)),
        ],
        compiler_params=pltpu.CompilerParams(
            collective_id=0, has_side_effects=True, vmem_limit_bytes=48 * 1024 * 1024),
        name="reduce_gradient",
    )(activations, cotangent)
    return out.reshape(2, 2 * half_cols)


def solution(mesh):
    placed = (P(("inner", "outer"), None), P(("inner", "outer"), None))
    return jax.shard_map(
        on_device,
        mesh=mesh,
        in_specs=placed,
        out_specs=P(("inner", "outer"), None),
        check_vma=False,
    )
```

time: 473 us -> 96.3 us (0.20)
  waiting for transfers between devices: 347 us -> 0 us
  Pallas kernels: 0 us -> 94.5 us
  matrix products: 44.3 us -> 0 us
  starting transfers between devices: 33.9 us -> 0 us
  other arithmetic: 27.8 us -> 0 us
  local copies, waits for them, and re-layouts: 19 us -> 1.66 us
    all_to_all x4 -> x0, waiting for transfers between devices: 347 us -> none  [the longest x1 326 us: on_device(): lax.all_to_all(coded.reshape(inner_count, group_rows, block_count, 128),...]
    pallas_call x0 -> x1, Pallas kernels: none -> 94.5 us  [on_device(): pl.pallas_call(kernel, out_shape=jax.ShapeDtypeStruct((2, 2 * half_blocks...]
    dot_general x3 -> x0, matrix products: 44.3 us -> none  [the longest x2 29.6 us: rotate(): jnp.einsum('rbk,kj->rbj', blocks, hadamard_matrix, precision=lax.Precisio...]
    all_to_all x4 -> x0, starting transfers between devices: 33.9 us -> none  [the longest x1 12.5 us: on_device(): lax.all_to_all(as_sent(group_scale.reshape(outer_count, owned_rows, block...]
    convert_element_type x4 -> x0, other arithmetic: 16.7 us -> none  [the longest x2 16.1 us: quantize(): jnp.clip(blocks / block_scale[..., None], -code_range, code_range)]
    reshape x1 -> x0, local copies, waits for them, and re-layouts: 14.8 us -> none  [on_device(): coded.reshape(inner_count, group_rows, block_count, 128)]
    reduce_sum x3 -> x0, other arithmetic: 11.1 us -> none  [the longest x1 10.4 us: combine_group(): partial_value = jnp.sum(dequantize(coded, block_scale), axis=0)]
  transfers between devices with their start and end apart: 4 -> 0, of which waited for: 3 -> 0; matrix products, arithmetic and copies ran while one was open for 7% -> 0% of each run, Pallas kernels for 0% -> 0%
where the time goes in v1:
time: 96.3 us; the launch traced here: 96.2 us
  Pallas kernels  94.5 us (98%)
  local copies, waits for them, and re-layouts  1.66 us (2%)
    pallas_call x1, Pallas kernels, on_device(): pl.pallas_call(kernel, out_shape=jax.ShapeDtypeStruct((2, 2 * half_blocks...  94.5 us

profile of v1, /device:TPU:1, one launch (start us, length us, event | category | flops | bytes accessed | tf_op | source)
XLA Modules:
  0.0 96.2 jit_solution(2869348895518867759)
XLA Ops:
  0.0 0.0 copy-start
  0.0 0.9 copy-done
  1.0 94.5 %reduce_gradient.1 = f32[2,112,128]{2,1,0:T(8,128)S(1)} custom-call(bf16[256,512]{1,0:T(8,128)(2,1)S(1)} %copy-done, bf16[256,14336]{1,0:T(8,128)(2,1)} %cot.1), custom_call_target="tpu_custom_call" | custom-call | tf_op jit(solution)/shard_map/reduce_gradient/pallas_call | solution.py:383
  95.5 0.7 copy.5
Async XLA Ops:
  0.0 0.9 copy-start

commit v2 on v1

v2 whole, which is shorter than its diff:
```python
import jax
import jax.numpy as jnp
from jax import lax
from jax.experimental import pallas as pl
from jax.experimental.pallas import tpu as pltpu
from jax.sharding import PartitionSpec as P

MESH = pl.DeviceIdType.MESH
epsilon = 1e-06
LANES = 128
y_jobs, y_width = 12, 4
z_jobs, z_width = 4, 2
z_period, x_lag, h_lag = 3, 1, 2
y_at = (0, 1, 2, 3, 4)
z_at = (0, 1, 2, 3, 4)
round_blocks = 8
y_per_round = round_blocks // y_width
y_rounds = y_jobs * y_width // round_blocks
rounds = y_rounds + z_jobs * z_width // round_blocks
half_blocks = y_jobs * y_width + z_jobs * z_width
half_cols = half_blocks * LANES
WY, WZ = y_width * LANES, z_width * LANES
TOK, ROWS = 256, 512
f32, bf16 = jnp.float32, jnp.bfloat16


def near(v):
    return v + 1 - 2 * lax.rem(v, 2)


def place(v, order):
    return jnp.where(v == order[0], 0, jnp.where(v == order[1], 1, jnp.where(v == order[2], 2, 3)))


def signs():
    r = lax.broadcasted_iota(jnp.int32, (256, 256), 0)
    q = lax.broadcasted_iota(jnp.int32, (256, 256), 1)
    common = r & q & 127
    common = common ^ (common >> 4)
    common = common ^ (common >> 2)
    common = common ^ (common >> 1)
    sign = (1 - 2 * (common & 1)).astype(f32)
    return jnp.where((r >> 7) == (q >> 7), sign, 0.0).astype(bf16)


def clipped(v):
    total = jnp.sum(v * v, axis=-1, keepdims=True)
    four = total * (4.0 / LANES) + 4.0 * LANES * epsilon
    bound = four * lax.rsqrt(four)
    return jnp.minimum(jnp.maximum(v, -bound), bound)


def each(n, f):
    def step(j, _):
        f(j)
        return 0
    lax.fori_loop(0, n, step, 0)


def kernel(act, cot, out, h2, at2, aown, asib, cy_own, cy_sib, cz_own, cz_sib, ch, ty, tz,
           ry1, ry2, ry3, ry4, rz1, rz2, rz3, rz4, part_y, part_z, coded_x, got_x, coded_h, got_h,
           s_loc, s_act, s_send, s_a, s_cot, s_y1, s_y2, s_y3, s_y4, s_z1, s_z2, s_z3, s_z4, s_x, s_h):
    i, o = lax.axis_index("inner"), lax.axis_index("outer")
    z, y, c = lax.div(i, 8), lax.rem(lax.div(i, 2), 4), lax.rem(i, 2)
    x, h = lax.div(o, 2), lax.rem(o, 2)
    yn, yf = near(y), 3 - y
    zn, zf = near(z), 3 - z

    def dev(z_, y_, c_, x_, h_):
        return (z_ * 8 + y_ * 2 + c_, x_ * 2 + h_)

    sib = dev(z, y, 1 - c, x, h)
    dev_yn, dev_yf = dev(z, yn, c, x, h), dev(z, yf, c, x, h)
    dev_zn, dev_zf = dev(zn, y, c, x, h), dev(zf, y, c, x, h)
    x_to = [lax.rem(x + d, 4) for d in (1, 2, 3)]
    h_to = [(c, 1 - h), (1 - c, h), (1 - c, 1 - h)]
    dev_x = [dev(z, y, c, to, h) for to in x_to]
    dev_h = [dev(z, y, c_, x, h_) for c_, h_ in h_to]

    barrier = pltpu.get_barrier_semaphore()
    for to in [dev_yn, dev_yf, dev_zn, dev_zf] + dev_x + dev_h:
        pl.semaphore_signal(barrier, inc=1, device_id=to, device_id_type=MESH)

    def send(src, dst, kind, got, to):
        return pltpu.make_async_remote_copy(
            src_ref=src, dst_ref=dst, send_sem=s_send.at[kind], recv_sem=got, device_id=to, device_id_type=MESH)

    def y_cols(half, j):
        return pl.ds(pl.multiple_of(half * half_cols + j * WY, LANES), WY)

    def z_cols(half, j):
        return pl.ds(pl.multiple_of(half * half_cols + y_jobs * WY + j * WZ, LANES), WZ)

    def load_y(j):
        return pltpu.make_async_copy(cot.at[:, y_cols(c, j)], cy_own.at[j], s_loc.at[j])

    def load_z(j):
        return pltpu.make_async_copy(cot.at[:, z_cols(c, j)], cz_own.at[j], s_loc.at[y_jobs + j])

    def lend_y(j):
        return send(cot.at[:, y_cols(1 - c, j)], cy_sib.at[j], 0, s_cot.at[j], sib)

    def lend_z(j):
        return send(cot.at[:, z_cols(1 - c, j)], cz_sib.at[j], 1, s_cot.at[y_jobs + j], sib)

    def start_loads(j):
        load_y(j).start()

        @pl.when(j < z_jobs)
        def _():
            load_z(j).start()

    def start_lends(j):
        lend_y(j).start()

        @pl.when(j < z_jobs)
        def _():
            lend_z(j).start()

    load_a = pltpu.make_async_copy(act, aown, s_act)
    load_a.start()
    each(y_jobs, start_loads)
    lend_a = send(act, asib, 2, s_a.at[0], sib)
    pl.semaphore_wait(barrier, 10)
    lend_a.start()
    each(y_jobs, start_lends)
    h2[...] = signs()

    def turn(which, a):
        t = a.astype(f32).T.astype(bf16)
        at2[which, :, 0:TOK] = t
        at2[which, :, TOK:2 * TOK] = t

    load_a.wait()
    turn(0, aown[...])
    lend_a.wait_recv()
    turn(1, asib[...])

    def rotate(which, block, width):
        for p in range(width // 256):
            cols = slice(p * 256, p * 256 + 256)
            v = jnp.dot(block[:, cols], h2[...], preferred_element_type=f32)
            hi = v.astype(bf16)
            ch[which, 0:TOK, cols] = hi
            ch[which, TOK:2 * TOK, cols] = (v - hi.astype(f32)).astype(bf16)

    def multiply(width, store):
        def rows(q, _):
            at = pl.ds(pl.multiple_of(q * 256, 256), 256)
            for p in range(width // 256):
                cols = slice(p * 256, p * 256 + 256)
                a = jnp.dot(at2[0, at, :], ch[0, :, cols], preferred_element_type=f32)
                b = jnp.dot(at2[1, at, :], ch[1, :, cols], preferred_element_type=f32)
                for k in range(2):
                    lanes = slice(k * LANES, k * LANES + LANES)
                    s = (clipped(a[:, lanes]) + clipped(b[:, lanes])).astype(bf16)
                    to = slice(p * 256 + k * LANES, p * 256 + k * LANES + LANES)
                    for zz in range(2):
                        zr = place(q * 2 + zz, (z, zf, zn))
                        for yy in range(4):
                            store(zr, yy, to, s[zz * 128 + yy * 32:zz * 128 + yy * 32 + 32])
            return 0

        lax.fori_loop(0, 2, rows, 0)

    def y1(j):
        return tuple(send(ty.at[j, k, pl.ds(2, 2)], ry1.at[j, k], 3, s_y1.at[j, k], to)
                     for k, to in enumerate((dev_yn, dev_yf)))

    def y2(j):
        return tuple(send(ty.at[j, k, 1], ry2.at[j, k], 4, s_y2.at[j, k], to)
                     for k, to in enumerate((dev_yf, dev_yn)))

    def y3(j):
        return send(ty.at[j, 1, 0], ry3.at[j], 5, s_y3.at[j], dev_zn)

    def y4(j):
        return send(ty.at[j, 0, 0, 1], ry4.at[j], 6, s_y4.at[j], dev_zf)

    def y_stage0(j):
        load_y(j).wait()
        rotate(0, cy_own.at[j], WY)
        lend_y(j).wait_recv()
        rotate(1, cy_sib.at[j], WY)

        def store(zr, yy, cols, rows):
            k = zr // 2
            yr = jnp.where(k == 0, place(yy, (y, yf, yn)), place(yy, (y, yn, yf)))
            ty[j, k, yr, zr % 2, :, cols] = rows

        multiply(WY, store)
        for cp in y1(j):
            cp.start()

    def y_stage1(j):
        first, second = y1(j), y2(j)
        for k in range(2):
            first[k].wait_recv()
            ty[j, k, 1] = ty[j, k, 1] + ry1[j, k, 1]
            second[k].start()
        for k in range(2):
            ty[j, k, 0] = ty[j, k, 0] + ry1[j, k, 0]

    def y_stage2(j):
        a, b = y2(j)
        b.wait_recv()
        ty[j, 1, 0] = ty[j, 1, 0] + ry2[j, 1]
        y3(j).start()
        a.wait_recv()
        ty[j, 0, 0] = ty[j, 0, 0] + ry2[j, 0]

    def y_stage3(j):
        y3(j).wait_recv()
        ty[j, 0, 0, 1] = ty[j, 0, 0, 1] + ry3[j, 1]
        y4(j).start()
        ty[j, 0, 0, 0] = ty[j, 0, 0, 0] + ry3[j, 0]

    def x_copies(g):
        return [send(coded_x.at[g, x_to[d]], got_x.at[g, d], 7, s_x.at[g], dev_x[d]) for d in range(3)]

    def send_round(g, part):
        for d in range(16):
            rows = [part[pl.ds(2 * d + e, round_blocks, stride=32), :] for e in range(2)]
            coded_x[g, (d % 8) // 2, d // 8, d % 2] = jnp.concatenate(rows, axis=0).astype(bf16)
        for cp in x_copies(g):
            cp.start()

    def y_stage4(j):
        y4(j).wait_recv()
        v = ty[j, 0, 0, 0].astype(f32) + ry4[j].astype(f32)
        for k in range(y_width):
            to = pl.multiple_of(lax.rem(j, y_per_round) * (y_width * 32) + k * 32, 32)
            part_y[pl.ds(to, 32), :] = clipped(v[:, k * LANES:(k + 1) * LANES])

        @pl.when(lax.rem(j, y_per_round) == y_per_round - 1)
        def _():
            send_round(lax.div(j, y_per_round), part_y)

    def z1(j):
        return send(tz.at[j, pl.ds(2, 2)], rz1.at[j], 8, s_z1.at[j], dev_zn)

    def z2(j):
        return send(tz.at[j, 1], rz2.at[j], 9, s_z2.at[j], dev_zf)

    def z3(j):
        return tuple(send(tz.at[j, 0, k, pl.ds(2, 2)], rz3.at[j, k], 10, s_z3.at[j, k], to)
                     for k, to in enumerate((dev_yn, dev_yf)))

    def z4(j):
        return tuple(send(tz.at[j, 0, k, 1], rz4.at[j, k], 11, s_z4.at[j, k], to)
                     for k, to in enumerate((dev_yf, dev_yn)))

    def z_stage0(j):
        load_z(j).wait()
        rotate(0, cz_own.at[j], WZ)
        lend_z(j).wait_recv()
        rotate(1, cz_sib.at[j], WZ)

        def store(zr, yy, cols, rows):
            tz[j, zr, 0, place(yy, (y, yf, yn)), :, cols] = rows[0:16]
            tz[j, zr, 1, place(yy, (y, yn, yf)), :, cols] = rows[16:32]

        multiply(WZ, store)
        z1(j).start()

    def z_stage1(j):
        z1(j).wait_recv()
        tz[j, 1] = tz[j, 1] + rz1[j, 1]
        z2(j).start()
        tz[j, 0] = tz[j, 0] + rz1[j, 0]

    def z_stage2(j):
        z2(j).wait_recv()
        tz[j, 0] = tz[j, 0] + rz2[j]
        for cp in z3(j):
            cp.start()

    def z_stage3(j):
        first, second = z3(j), z4(j)
        for k in range(2):
            first[k].wait_recv()
            tz[j, 0, k, 1] = tz[j, 0, k, 1] + rz3[j, k, 1]
            second[k].start()
        for k in range(2):
            tz[j, 0, k, 0] = tz[j, 0, k, 0] + rz3[j, k, 0]

    def z_stage4(j):
        for k, cp in enumerate(z4(j)):
            cp.wait_recv()
            v = tz[j, 0, k, 0].astype(f32) + rz4[j, k].astype(f32)
            for b in range(z_width):
                to = pl.multiple_of(j * (z_width * 32) + b * 32 + k * 16, 16)
                part_z[pl.ds(to, 16), :] = clipped(v[:, b * LANES:(b + 1) * LANES])

        @pl.when(j == z_jobs - 1)
        def _():
            send_round(y_rounds, part_z)

    def h_copies(g):
        return [send(coded_h.at[g, h_to[d][0] * 2 + h_to[d][1]], got_h.at[g, d], 12, s_h.at[g], dev_h[d])
                for d in range(3)]

    def wait_round(kind, g, got, sem):
        pltpu.make_async_copy(got.at[g], got.at[g], sem.at[g]).wait()

    def sum_x(g):
        wait_round(7, g, got_x, s_x)
        total = coded_x[g, x].astype(f32)
        for d in range(3):
            total = total + got_x[g, d].astype(f32)
        coded_h[g] = total.astype(bf16).reshape(4, 16, LANES)
        for cp in h_copies(g):
            cp.start()

    def finish(g):
        wait_round(12, g, got_h, s_h)
        for half, a, b in ((c, coded_h[g, c * 2 + h], got_h[g, 0]), (1 - c, got_h[g, 1], got_h[g, 2])):
            total = a.astype(f32) + b.astype(f32)
            hi = total.astype(bf16)
            rest = (total - hi.astype(f32)).astype(bf16)
            r = h2[0:LANES, 0:LANES]
            v = jnp.dot(hi, r, preferred_element_type=f32) + jnp.dot(rest, r, preferred_element_type=f32)
            v = v * (1.0 / LANES)
            to = pl.ds(pl.multiple_of(half * half_blocks + g * round_blocks, 8), round_blocks)
            out[0, to, :] = v[0:8]
            out[1, to, :] = v[8:16]

    y_stages = (y_stage0, y_stage1, y_stage2, y_stage3, y_stage4)
    z_stages = (z_stage0, z_stage1, z_stage2, z_stage3, z_stage4)
    y_sent = y_per_round - 1 + y_at[4]
    z_sent = (z_jobs - 1) * z_period + z_at[4]

    def tick(t, _):
        def at(first, period, jobs, f):
            since = t - first

            @pl.when((since >= 0) & (lax.rem(since, period) == 0) & (since < jobs * period))
            def _():
                f(lax.div(since, period))

        for k in range(5):
            at(y_at[k], 1, y_jobs, y_stages[k])
            at(z_at[k], z_period, z_jobs, z_stages[k])
        at(y_sent + x_lag, y_per_round, y_rounds, sum_x)
        at(z_sent + x_lag, 1, 1, lambda g: sum_x(y_rounds))
        at(z_sent + x_lag + h_lag, 1, 1, lambda g: finish(y_rounds))
        at(y_sent + x_lag + h_lag, y_per_round, y_rounds, finish)
        return 0

    lax.fori_loop(0, y_jobs + y_at[4] + x_lag + h_lag, tick, 0)

    for kind, ref in enumerate((cy_sib, cz_sib, asib, ty.at[:, :, pl.ds(2, 2)], ty.at[:, :, 1], ty.at[:, 1, 0],
                                ty.at[:, 0, 0, 1], coded_x.at[:, pl.ds(0, 3)], tz.at[:, pl.ds(2, 2)], tz.at[:, 1],
                                tz.at[:, 0, :, pl.ds(2, 2)], tz.at[:, 0, :, 1], coded_h.at[:, pl.ds(0, 3)])):
        pltpu.make_async_copy(ref, ref, s_send.at[kind]).wait()


def on_device(activations, cotangent):
    dma = pltpu.SemaphoreType.DMA
    vm = pltpu.VMEM
    ny, nz = y_jobs, z_jobs
    out = pl.pallas_call(
        kernel,
        out_shape=jax.ShapeDtypeStruct((2, 2 * half_blocks, LANES), f32),
        in_specs=[pl.BlockSpec(memory_space=pl.ANY)] * 2,
        out_specs=pl.BlockSpec(memory_space=pltpu.VMEM),
        scratch_shapes=[
            vm((256, 256), bf16),
            vm((2, ROWS, 2 * TOK), bf16),
            vm((TOK, ROWS), bf16), vm((TOK, ROWS), bf16),
            vm((ny, TOK, WY), bf16), vm((ny, TOK, WY), bf16),
            vm((nz, TOK, WZ), bf16), vm((nz, TOK, WZ), bf16),
            vm((2, 2 * TOK, max(WY, WZ)), bf16),
            vm((ny, 2, 4, 2, 32, WY), bf16),
            vm((nz, 4, 2, 4, 16, WZ), bf16),
            vm((ny, 2, 2, 2, 32, WY), bf16), vm((ny, 2, 2, 32, WY), bf16),
            vm((ny, 2, 32, WY), bf16), vm((ny, 32, WY), bf16),
            vm((nz, 2, 2, 4, 16, WZ), bf16), vm((nz, 2, 4, 16, WZ), bf16),
            vm((nz, 2, 2, 16, WZ), bf16), vm((nz, 2, 16, WZ), bf16),
            vm((32 * round_blocks, LANES), f32), vm((32 * round_blocks, LANES), f32),
            vm((rounds, 4, 2, 2, 16, LANES), bf16), vm((rounds, 3, 2, 2, 16, LANES), bf16),
            vm((rounds, 4, 16, LANES), bf16), vm((rounds, 3, 16, LANES), bf16),
            dma((ny + nz,)), dma, dma((13,)), dma((1,)), dma((ny + nz,)),
            dma((ny, 2)), dma((ny, 2)), dma((ny,)), dma((ny,)),
            dma((nz,)), dma((nz,)), dma((nz, 2)), dma((nz, 2)),
            dma((rounds,)), dma((rounds,)),
        ],
        compiler_params=pltpu.CompilerParams(
            collective_id=0, has_side_effects=True, vmem_limit_bytes=48 * 1024 * 1024),
        name="reduce_gradient",
    )(activations, cotangent)
    return out.reshape(2, 2 * half_cols)


def solution(mesh):
    placed = (P(("inner", "outer"), None), P(("inner", "outer"), None))
    return jax.shard_map(
        on_device,
        mesh=mesh,
        in_specs=placed,
        out_specs=P(("inner", "outer"), None),
        check_vma=False,
    )
```

time: 96.3 us -> 92.6 us (0.962)
  Pallas kernels: 94.5 us -> 90.9 us
    pallas_call x1, Pallas kernels: 94.5 us -> 90.9 us  [on_device(): pl.pallas_call(kernel, out_shape=jax.ShapeDtypeStruct((2, 2 * half_blocks...]
where the time goes in v2:
time: 92.6 us; the launch traced here: 92.5 us
  Pallas kernels  90.9 us (98%)
  local copies, waits for them, and re-layouts  1.66 us (2%)
    pallas_call x1, Pallas kernels, on_device(): pl.pallas_call(kernel, out_shape=jax.ShapeDtypeStruct((2, 2 * half_blocks...  90.9 us

profile of v2, /device:TPU:1, one launch (start us, length us, event | category | flops | bytes accessed | tf_op | source)
XLA Modules:
  0.0 92.5 jit_solution(10564138110044466460)
XLA Ops:
  0.0 0.0 copy-start
  0.0 0.9 %copy-done = bf16[256,512]{1,0:T(8,128)(2,1)S(1)} copy-done((bf16[256,512]{1,0:T(8,128)(2,1)S(1)}, bf16[256,512]{1,0:T(8,128)(2,1)}, u32[]{:S(2)}) %copy-start) | copy-done | bytes 262168
  1.0 90.9 %reduce_gradient.1 = f32[2,112,128]{2,1,0:T(8,128)S(1)} custom-call(bf16[256,512]{1,0:T(8,128)(2,1)S(1)} %copy-done, bf16[256,14336]{1,0:T(8,128)(2,1)} %cot.1), custom_call_target="tpu_custom_call" | custom-call | tf_op jit(solution)/shard_map/reduce_gradient/pallas_call | solution.py:362
  91.8 0.7 copy.5
Async XLA Ops:
  0.0 0.9 %copy-start = (bf16[256,512]{1,0:T(8,128)(2,1)S(1)}, bf16[256,512]{1,0:T(8,128)(2,1)}, u32[]{:S(2)}) copy-start(bf16[256,512]{1,0:T(8,128)(2,1)} %act.1) | copy-start | bytes 786436

commit v3 on v2

v3 whole, which is shorter than its diff:
```python
import jax
import jax.numpy as jnp
from jax import lax
from jax.experimental import pallas as pl
from jax.experimental.pallas import tpu as pltpu
from jax.sharding import PartitionSpec as P

MESH = pl.DeviceIdType.MESH
epsilon = 1e-06
LANES = 128
y_jobs = ((4, 2), (6, 2), (8, 2), (10, 2), (12, 2), (14, 2), (16, 2), (18, 2), (20, 2), (22, 2), (26, 2))
z_jobs = ((0, 1), (1, 1), (2, 1), (3, 1), (24, 1), (25, 1))
Y0, Y1, Y2, Y3, Y4, Z0, Z1, Z2, Z3, Z4, XS, HS, OUT = range(13)
steps = (
    (Y0, 4), (Z0, 3), (Y0, 3), (Y0, 1), (Z0, 0), (Z1, 3), (Z0, 5), (Y0, 2), (Z0, 1), (Y1, 3), (Z1, 0),
    (Y1, 1), (Y1, 2), (Y0, 0), (Z0, 4), (Y0, 6), (Y2, 1), (Y1, 4), (Y0, 7), (Z1, 1), (Z0, 2), (Z1, 5),
    (Y2, 2), (Y3, 1), (Y0, 5), (Y1, 0), (Y2, 4), (Z1, 2), (Y2, 3), (Y0, 8), (Z2, 1), (Y1, 5), (Y1, 7),
    (Z1, 4), (Y1, 6), (Y2, 0), (Z2, 0), (Y0, 9), (Y3, 4), (Y2, 5), (Y3, 0), (Y1, 8), (Y4, 1), (Y3, 3),
    (Y4, 4), (Y2, 7), (Y3, 2), (Y0, 10), (Y2, 6), (Y3, 5), (Y4, 3), (Y1, 9), (Y2, 8), (Y4, 2), (Y4, 0),
    (Z2, 3), (Y3, 7), (Y3, 6), (Y1, 10), (Z2, 2), (Z2, 5), (Y3, 8), (XS, 2), (Y4, 5), (Y2, 9), (Z2, 4),
    (XS, 3), (Z3, 3), (XS, 1), (Y4, 7), (Z3, 1), (Y2, 10), (Y4, 6), (Z3, 5), (XS, 4), (Y3, 9), (Z3, 4),
    (Z3, 2), (Z4, 3), (Z3, 0), (HS, 3), (Z4, 1), (Y3, 10), (Z4, 4), (Z4, 2), (Z4, 0), (HS, 4), (XS, 0),
    (Y4, 9), (HS, 1), (Y4, 8), (XS, 5), (Z4, 5), (Y4, 10), (XS, 6), (OUT, 3), (HS, 2), (HS, 0), (HS, 5),
    (HS, 6), (OUT, 1), (OUT, 2), (OUT, 0), (OUT, 4), (OUT, 5), (OUT, 6),
)
pairs = 28
z_first = [sum(n for _, n in z_jobs[:j]) for j in range(len(z_jobs))]
rounds = pairs // 4
half_cols = pairs * 256
TOK, ROWS = 256, 512
f32, bf16 = jnp.float32, jnp.bfloat16


def near(v):
    return v + 1 - 2 * lax.rem(v, 2)


def place(v, order):
    return jnp.where(v == order[0], 0, jnp.where(v == order[1], 1, jnp.where(v == order[2], 2, 3)))


def signs():
    r = lax.broadcasted_iota(jnp.int32, (256, 256), 0)
    q = lax.broadcasted_iota(jnp.int32, (256, 256), 1)
    common = r & q & 127
    common = common ^ (common >> 4)
    common = common ^ (common >> 2)
    common = common ^ (common >> 1)
    sign = (1 - 2 * (common & 1)).astype(f32)
    return jnp.where((r >> 7) == (q >> 7), sign, 0.0).astype(bf16)


def clipped(v):
    total = jnp.sum(v * v, axis=-1, keepdims=True)
    four = total * (4.0 / LANES) + 4.0 * LANES * epsilon
    bound = four * lax.rsqrt(four)
    return jnp.minimum(jnp.maximum(v, -bound), bound)


def each(n, f):
    def step(j, _):
        f(j)
        return 0
    lax.fori_loop(0, n, step, 0)


def kernel(act, cot, out, h2, at2, aown, asib, c_own, c_sib, ch, ty, tz,
           ry1, ry2, ry3, ry4, rz1, rz2, rz3, rz4, part, coded_x, got_x, coded_h, got_h,
           s_loc, s_act, s_send, s_a, s_cot, s_y1, s_y2, s_y3, s_y4, s_z1, s_z2, s_z3, s_z4, s_x, s_h):
    i, o = lax.axis_index("inner"), lax.axis_index("outer")
    z, y, c = lax.div(i, 8), lax.rem(lax.div(i, 2), 4), lax.rem(i, 2)
    x, h = lax.div(o, 2), lax.rem(o, 2)
    yn, yf = near(y), 3 - y
    zn, zf = near(z), 3 - z

    def dev(z_, y_, c_, x_, h_):
        return (z_ * 8 + y_ * 2 + c_, x_ * 2 + h_)

    sib = dev(z, y, 1 - c, x, h)
    dev_yn, dev_yf = dev(z, yn, c, x, h), dev(z, yf, c, x, h)
    dev_zn, dev_zf = dev(zn, y, c, x, h), dev(zf, y, c, x, h)
    x_to = [lax.rem(x + d, 4) for d in (1, 2, 3)]
    h_to = [(c, 1 - h), (1 - c, h), (1 - c, 1 - h)]
    dev_x = [dev(z, y, c, to, h) for to in x_to]
    dev_h = [dev(z, y, c_, x, h_) for c_, h_ in h_to]

    barrier = pltpu.get_barrier_semaphore()
    for to in [dev_yn, dev_yf, dev_zn, dev_zf] + dev_x + dev_h:
        pl.semaphore_signal(barrier, inc=1, device_id=to, device_id_type=MESH)

    def send(src, dst, kind, got, to):
        return pltpu.make_async_remote_copy(
            src_ref=src, dst_ref=dst, send_sem=s_send.at[kind], recv_sem=got, device_id=to, device_id_type=MESH)

    def columns(half, p, n):
        return pl.ds(pl.multiple_of(half * half_cols + p * 256, LANES), n * 256)

    def load(p, n):
        return pltpu.make_async_copy(cot.at[:, columns(c, p, n)], c_own.at[:, columns(0, p, n)], s_loc.at[p])

    def lend(p, n):
        return send(cot.at[:, columns(1 - c, p, n)], c_sib.at[:, columns(0, p, n)], 0, s_cot.at[p], sib)

    first_use = [y_jobs[j] if s == Y0 else z_jobs[j] for s, j in steps if s in (Y0, Z0)]
    load_a = pltpu.make_async_copy(act, aown, s_act)
    load_a.start()
    for p, n in first_use:
        load(p, n).start()
    lend_a = send(act, asib, 1, s_a.at[0], sib)
    pl.semaphore_wait(barrier, 10)
    lend_a.start()
    for p, n in first_use:
        lend(p, n).start()
    h2[...] = signs()

    def turn(which, a):
        t = a.astype(f32).T.astype(bf16)
        at2[which, :, 0:TOK] = t
        at2[which, :, TOK:2 * TOK] = t

    load_a.wait()
    turn(0, aown[...])
    lend_a.wait_recv()
    turn(1, asib[...])

    places_z = [place(v, (z, zf, zn)) for v in range(4)]

    def compute(p, n, store):
        for q in range(n):
            for which, block in enumerate((c_own, c_sib)):
                v = jnp.dot(block[:, columns(0, p + q, 1)], h2[...], preferred_element_type=f32)
                hi = v.astype(bf16)
                ch[which, q, 0:TOK, :] = hi
                ch[which, q, TOK:2 * TOK, :] = (v - hi.astype(f32)).astype(bf16)
        for r in range(2):
            at = slice(r * 256, r * 256 + 256)
            for q in range(n):
                a = jnp.dot(at2[0, at, :], ch[0, q], preferred_element_type=f32)
                b = jnp.dot(at2[1, at, :], ch[1, q], preferred_element_type=f32)
                for k in range(2):
                    lanes = slice(k * LANES, k * LANES + LANES)
                    s = (clipped(a[:, lanes]) + clipped(b[:, lanes])).astype(bf16)
                    for zz in range(2):
                        for yy in range(4):
                            store(q, k, places_z[r * 2 + zz], yy, s[zz * 128 + yy * 32:zz * 128 + yy * 32 + 32])

    place_a = [place(v, (y, yf, yn)) for v in range(4)]
    place_b = [place(v, (y, yn, yf)) for v in range(4)]

    def y1(j):
        ps = pl.ds(*y_jobs[j])
        return tuple(send(ty.at[ps, k, pl.ds(2, 2)], ry1.at[ps, k], 2, s_y1.at[j, k], to)
                     for k, to in enumerate((dev_yn, dev_yf)))

    def y2(j):
        ps = pl.ds(*y_jobs[j])
        return tuple(send(ty.at[ps, k, 1], ry2.at[ps, k], 3, s_y2.at[j, k], to)
                     for k, to in enumerate((dev_yf, dev_yn)))

    def y3(j):
        ps = pl.ds(*y_jobs[j])
        return send(ty.at[ps, 1, 0], ry3.at[ps], 4, s_y3.at[j], dev_zn)

    def y4(j):
        ps = pl.ds(*y_jobs[j])
        return send(ty.at[ps, 0, 0, 1], ry4.at[ps], 5, s_y4.at[j], dev_zf)

    def y_compute(p, n):
        def store(q, k, zr, yy, rows):
            second = lax.div(zr, 2)
            yr = jnp.where(second == 0, place_a[yy], place_b[yy])
            ty[p + q, second, yr, lax.rem(zr, 2), :, k * LANES:(k + 1) * LANES] = rows

        compute(p, n, store)

    def y_stage0(j):
        for cp in y1(j):
            cp.start()

    def y_stage1(j):
        ps = pl.ds(*y_jobs[j])
        first, second = y1(j), y2(j)
        for k in range(2):
            first[k].wait_recv()
            ty[ps, k, 1] = ty[ps, k, 1] + ry1[ps, k, 1]
            second[k].start()
        for k in range(2):
            ty[ps, k, 0] = ty[ps, k, 0] + ry1[ps, k, 0]

    def y_stage2(j):
        ps = pl.ds(*y_jobs[j])
        a, b = y2(j)
        b.wait_recv()
        ty[ps, 1, 0] = ty[ps, 1, 0] + ry2[ps, 1]
        y3(j).start()
        a.wait_recv()
        ty[ps, 0, 0] = ty[ps, 0, 0] + ry2[ps, 0]

    def y_stage3(j):
        ps = pl.ds(*y_jobs[j])
        y3(j).wait_recv()
        ty[ps, 0, 0, 1] = ty[ps, 0, 0, 1] + ry3[ps, 1]
        y4(j).start()
        ty[ps, 0, 0, 0] = ty[ps, 0, 0, 0] + ry3[ps, 0]

    def keep_part(p, k, v):
        at = (p % 4 * 2 + k) * 32
        part[p // 4, at:at + 32, :] = clipped(v)

    def y_stage4(j):
        y4(j).wait_recv()
        first, n = y_jobs[j]
        for p in range(first, first + n):
            v = ty[p, 0, 0, 0].astype(f32) + ry4[p].astype(f32)
            for k in range(2):
                keep_part(p, k, v[:, k * LANES:(k + 1) * LANES])

    def zp(j):
        return pl.ds(z_first[j], z_jobs[j][1])

    def z1(j):
        return send(tz.at[zp(j), pl.ds(2, 2)], rz1.at[zp(j)], 6, s_z1.at[j], dev_zn)

    def z2(j):
        return send(tz.at[zp(j), 1], rz2.at[zp(j)], 7, s_z2.at[j], dev_zf)

    def z3(j):
        return tuple(send(tz.at[zp(j), 0, k, pl.ds(2, 2)], rz3.at[zp(j), k], 8, s_z3.at[j, k], to)
                     for k, to in enumerate((dev_yn, dev_yf)))

    def z4(j):
        return tuple(send(tz.at[zp(j), 0, k, 1], rz4.at[zp(j), k], 9, s_z4.at[j, k], to)
                     for k, to in enumerate((dev_yf, dev_yn)))

    def z_compute(m, p, n):
        def store(q, k, zr, yy, rows):
            tz[m + q, zr, k, (place_a, place_b)[k][yy]] = rows

        compute(p, n, store)

    def z_stage0(j):
        z1(j).start()

    def z_stage1(j):
        ps = zp(j)
        z1(j).wait_recv()
        tz[ps, 1] = tz[ps, 1] + rz1[ps, 1]
        z2(j).start()
        tz[ps, 0] = tz[ps, 0] + rz1[ps, 0]

    def z_stage2(j):
        ps = zp(j)
        z2(j).wait_recv()
        tz[ps, 0] = tz[ps, 0] + rz2[ps]
        for cp in z3(j):
            cp.start()

    def z_stage3(j):
        ps = zp(j)
        first, second = z3(j), z4(j)
        for k in range(2):
            first[k].wait_recv()
            tz[ps, 0, k, 1] = tz[ps, 0, k, 1] + rz3[ps, k, 1]
            second[k].start()
        for k in range(2):
            tz[ps, 0, k, 0] = tz[ps, 0, k, 0] + rz3[ps, k, 0]

    def z_stage4(j):
        for k, cp in enumerate(z4(j)):
            cp.wait_recv()
            for q in range(z_jobs[j][1]):
                m = z_first[j] + q
                keep_part(z_jobs[j][0] + q, k, tz[m, 0, k, 0].astype(f32) + rz4[m, k].astype(f32))

    def x_copies(g):
        return [send(coded_x.at[g, x_to[d]], got_x.at[g, d], 10, s_x.at[g], dev_x[d]) for d in range(3)]

    def h_copies(g):
        return [send(coded_h.at[g, h_to[d][0] * 2 + h_to[d][1]], got_h.at[g, d], 11, s_h.at[g], dev_h[d])
                for d in range(3)]

    def send_x(g):
        for d in range(16):
            rows = [part[g, pl.ds(2 * d + e, 8, stride=32), :] for e in range(2)]
            coded_x[g, (d % 8) // 2, d // 8, d % 2] = jnp.concatenate(rows, axis=0).astype(bf16)
        for cp in x_copies(g):
            cp.start()

    def sum_x(g):
        pltpu.make_async_copy(got_x.at[g], got_x.at[g], s_x.at[g]).wait()
        total = coded_x[g, x].astype(f32)
        for d in range(3):
            total = total + got_x[g, d].astype(f32)
        coded_h[g] = total.astype(bf16).reshape(4, 16, LANES)
        for cp in h_copies(g):
            cp.start()

    def finish(g):
        pltpu.make_async_copy(got_h.at[g], got_h.at[g], s_h.at[g]).wait()
        for half, a, b in ((c, coded_h[g, c * 2 + h], got_h[g, 0]), (1 - c, got_h[g, 1], got_h[g, 2])):
            total = a.astype(f32) + b.astype(f32)
            hi = total.astype(bf16)
            rest = (total - hi.astype(f32)).astype(bf16)
            r = h2[0:LANES, 0:LANES]
            v = jnp.dot(hi, r, preferred_element_type=f32) + jnp.dot(rest, r, preferred_element_type=f32)
            v = v * (1.0 / LANES)
            to = pl.ds(pl.multiple_of(half * (2 * pairs) + g * 8, 8), 8)
            out[0, to, :] = v[0:8]
            out[1, to, :] = v[8:16]

    run = (y_stage0, y_stage1, y_stage2, y_stage3, y_stage4, z_stage0, z_stage1, z_stage2, z_stage3, z_stage4,
           send_x, sum_x, finish)
    starts = [k for k, (stage, _) in enumerate(steps) if stage in (Y0, Z0)] + [len(steps)]
    assert starts[0] == 0
    turns = len(starts) - 1
    sort = [(0 if steps[k][0] == Y0 else 2) + (2 - n) for k, (_, n) in zip(starts, first_use)]
    place_of = [z_first[steps[k][1]] if steps[k][0] == Z0 else 0 for k in starts[:-1]]

    def pick(t, values):
        at = jnp.int32(values[0])
        for k, v in enumerate(values):
            if v != values[0]:
                at = jnp.where(t == k, v, at)
        return at

    def inputs(k):
        load(*first_use[k]).wait()
        lend(*first_use[k]).wait_recv()

    def turn_of(t):
        first, now, m = pick(t, [p for p, _ in first_use]), pick(t, sort), pick(t, place_of)
        for kind in sorted(set(sort)):
            @pl.when(now == kind)
            def _():
                if kind < 2:
                    y_compute(first, 2 - kind)
                else:
                    z_compute(m, first, 4 - kind)

        def among(a, b):
            if b - a > 1:
                mid = (a + b) // 2
                pl.when(t < mid)(lambda: among(a, mid))
                pl.when(t >= mid)(lambda: among(mid, b))
                return
            for stage, j in steps[starts[a]:starts[b]]:
                run[stage](j)
            if b < turns:
                inputs(b)

        among(0, turns)

    inputs(0)
    each(turns, turn_of)

    once = [(0, c_sib), (1, asib), (6, tz.at[:, pl.ds(2, 2)]), (7, tz.at[:, 1]), (8, tz.at[:, 0, :, pl.ds(2, 2)]),
            (9, tz.at[:, 0, :, 1]), (10, coded_x.at[:, pl.ds(0, 3)]), (11, coded_h.at[:, pl.ds(0, 3)])]
    ny = sum(n for _, n in y_jobs)
    once += [(2, ty.at[0:ny, :, pl.ds(2, 2)]), (3, ty.at[0:ny, :, 1]), (4, ty.at[0:ny, 1, 0]),
             (5, ty.at[0:ny, 0, 0, 1])]
    for kind, ref in once:
        pltpu.make_async_copy(ref, ref, s_send.at[kind]).wait()


def on_device(activations, cotangent):
    dma = pltpu.SemaphoreType.DMA
    vm = pltpu.VMEM
    ny, nz = len(y_jobs), len(z_jobs)
    nzp = sum(n for _, n in z_jobs)
    out = pl.pallas_call(
        kernel,
        out_shape=jax.ShapeDtypeStruct((2, 4 * pairs, LANES), f32),
        in_specs=[pl.BlockSpec(memory_space=pl.ANY)] * 2,
        out_specs=pl.BlockSpec(memory_space=pltpu.VMEM),
        scratch_shapes=[
            vm((256, 256), bf16),
            vm((2, ROWS, 2 * TOK), bf16),
            vm((TOK, ROWS), bf16), vm((TOK, ROWS), bf16),
            vm((TOK, half_cols), bf16), vm((TOK, half_cols), bf16),
            vm((2, 2, 2 * TOK, 256), bf16),
            vm((pairs, 2, 4, 2, 32, 256), bf16),
            vm((nzp, 4, 2, 4, 32, LANES), bf16),
            vm((pairs, 2, 2, 2, 32, 256), bf16), vm((pairs, 2, 2, 32, 256), bf16),
            vm((pairs, 2, 32, 256), bf16), vm((pairs, 32, 256), bf16),
            vm((nzp, 2, 2, 4, 32, LANES), bf16), vm((nzp, 2, 4, 32, LANES), bf16),
            vm((nzp, 2, 2, 32, LANES), bf16), vm((nzp, 2, 32, LANES), bf16),
            vm((rounds, 256, LANES), f32),
            vm((rounds, 4, 2, 2, 16, LANES), bf16), vm((rounds, 3, 2, 2, 16, LANES), bf16),
            vm((rounds, 4, 16, LANES), bf16), vm((rounds, 3, 16, LANES), bf16),
            dma((pairs,)), dma, dma((12,)), dma((1,)), dma((pairs,)),
            dma((ny, 2)), dma((ny, 2)), dma((ny,)), dma((ny,)),
            dma((nz,)), dma((nz,)), dma((nz, 2)), dma((nz, 2)),
            dma((rounds,)), dma((rounds,)),
        ],
        compiler_params=pltpu.CompilerParams(
            collective_id=0, has_side_effects=True, vmem_limit_bytes=48 * 1024 * 1024),
        name="reduce_gradient",
    )(activations, cotangent)
    return out.reshape(2, 2 * half_cols)


def solution(mesh):
    placed = (P(("inner", "outer"), None), P(("inner", "outer"), None))
    return jax.shard_map(
        on_device,
        mesh=mesh,
        in_specs=placed,
        out_specs=P(("inner", "outer"), None),
        check_vma=False,
    )
```

time: 92.6 us -> 82 us (0.89)
  Pallas kernels: 90.9 us -> 80.3 us
    pallas_call x1, Pallas kernels: 90.9 us -> 80.3 us  [on_device(): pl.pallas_call(kernel, out_shape=jax.ShapeDtypeStruct((2, 4 * pairs, LANE...]
where the time goes in v3:
time: 82 us; the launch traced here: 81.9 us
  Pallas kernels  80.3 us (98%)
  local copies, waits for them, and re-layouts  1.66 us (2%)
    pallas_call x1, Pallas kernels, on_device(): pl.pallas_call(kernel, out_shape=jax.ShapeDtypeStruct((2, 4 * pairs, LANE...  80.3 us
    unnamed x3, local copies, waits for them, and re-layouts  1.66 us

profile of v3, /device:TPU:1, one launch (start us, length us, event | category | flops | bytes accessed | tf_op | source)
XLA Modules:
  0.0 81.9 jit_solution(14984627676252934814)
XLA Ops:
  0.0 0.0 copy-start
  0.0 0.9 %copy-done = bf16[256,512]{1,0:T(8,128)(2,1)S(1)} copy-done((bf16[256,512]{1,0:T(8,128)(2,1)S(1)}, bf16[256,512]{1,0:T(8,128)(2,1)}, u32[]{:S(2)}) %copy-start) | copy-done | bytes 262168
  1.0 80.3 %reduce_gradient.1 = f32[2,112,128]{2,1,0:T(8,128)S(1)} custom-call(bf16[256,512]{1,0:T(8,128)(2,1)S(1)} %copy-done, bf16[256,14336]{1,0:T(8,128)(2,1)} %cot.1), custom_call_target="tpu_custom_call" | custom-call | tf_op jit(solution)/shard_map/reduce_gradient/pallas_call | solution.py:370
  81.2 0.7 copy.5
Async XLA Ops:
  0.0 0.9 %copy-start = (bf16[256,512]{1,0:T(8,128)(2,1)S(1)}, bf16[256,512]{1,0:T(8,128)(2,1)}, u32[]{:S(2)}) copy-start(bf16[256,512]{1,0:T(8,128)(2,1)} %act.1) | copy-start | bytes 786436

commit v4 on v3

--- a/solution.py
+++ b/solution.py
@@ -12,16 +12,16 @@
 z_jobs = ((0, 1), (1, 1), (2, 1), (3, 1), (24, 1), (25, 1))
 Y0, Y1, Y2, Y3, Y4, Z0, Z1, Z2, Z3, Z4, XS, HS, OUT = range(13)
 steps = (
-    (Y0, 4), (Z0, 3), (Y0, 3), (Y0, 1), (Z0, 0), (Z1, 3), (Z0, 5), (Y0, 2), (Z0, 1), (Y1, 3), (Z1, 0),
-    (Y1, 1), (Y1, 2), (Y0, 0), (Z0, 4), (Y0, 6), (Y2, 1), (Y1, 4), (Y0, 7), (Z1, 1), (Z0, 2), (Z1, 5),
-    (Y2, 2), (Y3, 1), (Y0, 5), (Y1, 0), (Y2, 4), (Z1, 2), (Y2, 3), (Y0, 8), (Z2, 1), (Y1, 5), (Y1, 7),
-    (Z1, 4), (Y1, 6), (Y2, 0), (Z2, 0), (Y0, 9), (Y3, 4), (Y2, 5), (Y3, 0), (Y1, 8), (Y4, 1), (Y3, 3),
-    (Y4, 4), (Y2, 7), (Y3, 2), (Y0, 10), (Y2, 6), (Y3, 5), (Y4, 3), (Y1, 9), (Y2, 8), (Y4, 2), (Y4, 0),
-    (Z2, 3), (Y3, 7), (Y3, 6), (Y1, 10), (Z2, 2), (Z2, 5), (Y3, 8), (XS, 2), (Y4, 5), (Y2, 9), (Z2, 4),
-    (XS, 3), (Z3, 3), (XS, 1), (Y4, 7), (Z3, 1), (Y2, 10), (Y4, 6), (Z3, 5), (XS, 4), (Y3, 9), (Z3, 4),
-    (Z3, 2), (Z4, 3), (Z3, 0), (HS, 3), (Z4, 1), (Y3, 10), (Z4, 4), (Z4, 2), (Z4, 0), (HS, 4), (XS, 0),
-    (Y4, 9), (HS, 1), (Y4, 8), (XS, 5), (Z4, 5), (Y4, 10), (XS, 6), (OUT, 3), (HS, 2), (HS, 0), (HS, 5),
-    (HS, 6), (OUT, 1), (OUT, 2), (OUT, 0), (OUT, 4), (OUT, 5), (OUT, 6),
+    (Y0, 0), (Z0, 2), (Y0, 1), (Z0, 1), (Y0, 2), (Z0, 3), (Y1, 0), (Y0, 4), (Z0, 4), (Z1, 1), (Y1, 1),
+    (Z0, 0), (Z1, 3), (Y2, 0), (Y1, 2), (Y0, 3), (Y0, 5), (Y1, 4), (Z1, 0), (Y2, 2), (Y0, 8), (Y1, 3),
+    (Y3, 0), (Y2, 1), (Y0, 7), (Z1, 2), (Y0, 6), (Y2, 4), (Y1, 5), (Z2, 3), (Y3, 1), (Y2, 3), (Y3, 2),
+    (Z1, 4), (Z0, 5), (Y3, 4), (Y1, 7), (Y3, 3), (Y0, 9), (Y1, 8), (Y1, 6), (Y0, 10), (Y2, 5), (Y4, 0),
+    (Y4, 1), (Z2, 0), (Z1, 5), (Y1, 9), (Z2, 2), (Y2, 7), (Y3, 5), (Z2, 1), (Y4, 2), (Y4, 4), (XS, 1),
+    (Y2, 6), (Y3, 7), (Y4, 3), (Y2, 8), (Y1, 10), (Y3, 6), (Z2, 4), (Z3, 0), (Z3, 3), (Y2, 9), (Z2, 5),
+    (Y3, 8), (Y4, 7), (Z3, 1), (Y2, 10), (Y4, 5), (Z3, 2), (Z4, 0), (Z4, 3), (Z3, 5), (Y3, 9), (XS, 2),
+    (Z3, 4), (Y4, 6), (HS, 1), (Z4, 1), (Z4, 2), (Y3, 10), (Z4, 5), (Y4, 8), (XS, 0), (XS, 4), (Y4, 9),
+    (XS, 5), (Z4, 4), (HS, 2), (XS, 3), (Y4, 10), (XS, 6), (OUT, 1), (HS, 0), (HS, 4), (HS, 3), (HS, 5),
+    (HS, 6), (OUT, 0), (OUT, 2), (OUT, 4), (OUT, 3), (OUT, 5), (OUT, 6),
 )
 pairs = 28
 z_first = [sum(n for _, n in z_jobs[:j]) for j in range(len(z_jobs))]
@@ -370,7 +370,7 @@
     out = pl.pallas_call(
         kernel,
         out_shape=jax.ShapeDtypeStruct((2, 4 * pairs, LANES), f32),
-        in_specs=[pl.BlockSpec(memory_space=pl.ANY)] * 2,
+        in_specs=[pl.BlockSpec(memory_space=pltpu.HBM)] * 2,
         out_specs=pl.BlockSpec(memory_space=pltpu.VMEM),
         scratch_shapes=[
             vm((256, 256), bf16),
@@ -393,7 +393,7 @@
             dma((rounds,)), dma((rounds,)),
         ],
         compiler_params=pltpu.CompilerParams(
-            collective_id=0, has_side_effects=True, vmem_limit_bytes=48 * 1024 * 1024),
+            collective_id=0, has_side_effects=True, vmem_limit_bytes=64 * 1024 * 1024 - 10560 * 1024),
         name="reduce_gradient",
     )(activations, cotangent)
     return out.reshape(2, 2 * half_cols)

time: 82 us -> 81.2 us (level)
  local copies, waits for them, and re-layouts: 1.66 us -> 0.71 us
    unnamed x3 -> x1, local copies, waits for them, and re-layouts: 1.66 us -> 0.71 us
where the time goes in v4:
time: 81.2 us; the launch traced here: 81.1 us
  Pallas kernels  80.4 us (99%)
    pallas_call x1, Pallas kernels, on_device(): pl.pallas_call(kernel, out_shape=jax.ShapeDtypeStruct((2, 4 * pairs, LANE...  80.4 us

profile of v4, /device:TPU:1, one launch (start us, length us, event | category | flops | bytes accessed | tf_op | source)
XLA Modules:
  0.0 81.1 jit_solution(12350497003234752999)
XLA Ops:
  0.0 80.4 %reduce_gradient.1 = f32[2,112,128]{2,1,0:T(8,128)S(1)} custom-call(bf16[256,512]{1,0:T(8,128)(2,1)} %act.1, bf16[256,14336]{1,0:T(8,128)(2,1)} %cot.1), custom_call_target="tpu_custom_call" | custom-call | tf_op jit(solution)/shard_map/reduce_gradient/pallas_call | solution.py:370
  80.4 0.7 copy.5
